TPU v7x, 256 devices: a whole 4x4x8 slice. The times are simulated.
256 devices in a mesh: rows: 32 (over z, x), cols: 8 (over y, core).
Axes of the slice: x: 4, y: 4, z: 8, core: 2. Of those that a mesh axis runs over, the one named last changes fastest.
Arguments:
- points: float32 [16, 262144], P(None, ('rows', 'cols')), may hold values from -6 to 6
- lengthscales: float32 [16], replicated, may hold values from 2 to 3
- targets: float32 [64, 262144], P(None, ('rows', 'cols')), may hold values from -6 to 6
- inducing_weights: bfloat16 [64, 2048], P(None, 'cols'), may hold values from -0.59765625 to 0.59765625
- inducing_index: int32 [2048], replicated, may hold values from 0 to 262143
- block_order: int32 [3], replicated, may hold values from 0 to 255
- block_inverse: bfloat16 [256, 1024, 1024], P(('rows', 'cols')), may hold values from -0.1 to 0.1
Outputs:
- residual: float32 [64, 262144], P(None, ('rows', 'cols'))
- weights: float32 [64, 262144], P(None, ('rows', 'cols'))
All inputs are finite; a program needn't handle non-finite values.
Results may differ from a plain program's by a relative error of at most 0.00095.
The roundings to bfloat16 on the way count: a program that leaves them out, or rounds other values in their place, can miss the bound.
Values may be sent and summed in bfloat16 or wider, within the bound.
A program may use at most 64 MiB of HBM per device.

v0:
```python
import math

import jax
import jax.numpy as jnp
from jax import lax
from jax.sharding import PartitionSpec as P

noise_var = 0.5


def broadcast(value, axis, root):
    mine = lax.axis_index(axis) == root
    return lax.psum(jnp.where(mine, value, jnp.zeros_like(value)), axis)


def kernel_tile(left, right):
    crossed = lax.dot_general(
        left,
        right,
        (((0,), (0,)), ((), ())),
        precision=lax.Precision.HIGHEST,
        preferred_element_type=jnp.float32,
    )
    left_sq = jnp.sum(left * left, axis=0)
    right_sq = jnp.sum(right * right, axis=0)
    return jnp.exp(-0.5 * (left_sq[:, None] + right_sq[None, :] - 2.0 * crossed)).astype(
        jnp.bfloat16
    )


def spread_step(candidate, owner_id):
    return broadcast(candidate, ("rows", "cols"), owner_id)


def body(
    points, lengthscales, targets, inducing_weights, inducing_index, block_order, block_inverse
):
    points_dev = points.shape[1]
    per_device = block_inverse.shape[0]
    step_count = block_order.shape[0]
    device_id = lax.axis_index(("rows", "cols"))
    scaled = points / lengthscales[:, None]
    owners = block_order // per_device
    slots = block_order % per_device
    local_index = inducing_index - device_id * points_dev
    inside = (local_index >= 0) & (local_index < points_dev)
    picked = jnp.take(scaled, jnp.clip(local_index, 0, points_dev - 1), axis=1)
    masked = jnp.where(inside[None, :], picked, 0.0)
    own_blocks = []
    for step_no in range(step_count):
        own_coords = scaled
        own_blocks.append(jnp.where(owners[step_no] == device_id, own_coords, 0.0))
    summed = lax.psum(masked, ("rows", "cols"))
    start_sum = jnp.zeros((targets.shape[0], points_dev), jnp.float32)
    running = start_sum
    shard_part = lax.all_gather(inducing_weights, "cols", axis=1, tiled=True)
    columns = shard_part.shape[1]
    sub_len = math.gcd(columns, 512)
    for part_no in range(columns // sub_len):
        coords = lax.dynamic_slice_in_dim(summed, part_no * sub_len, sub_len, 1)
        tile = kernel_tile(coords, scaled)
        running = running + jnp.dot(
            shard_part[:, part_no * sub_len : (part_no + 1) * sub_len],
            tile,
            preferred_element_type=jnp.float32,
        )
    residual = targets - running
    weights = jnp.zeros_like(residual)
    for step_no in range(step_count):
        owner_id = owners[step_no]
        slot_id = slots[step_no]
        shifted = residual.astype(jnp.bfloat16)
        candidate = jnp.dot(
            shifted, block_inverse[slot_id], preferred_element_type=jnp.float32
        ).astype(jnp.bfloat16)
        delta = spread_step(candidate, owner_id)
        own_coords = scaled
        block_coords = broadcast(own_coords, ("rows", "cols"), owner_id)
        residual = residual - jnp.dot(
            delta, kernel_tile(block_coords, scaled), preferred_element_type=jnp.float32
        )
        delta_f = delta.astype(jnp.float32)
        is_owner = owner_id == device_id
        block_res = residual
        residual = jnp.where(is_owner, block_res - noise_var * delta_f, block_res)
        block_wts = weights
        weights = jnp.where(is_owner, block_wts + delta_f, block_wts)
    return (residual, weights)


def solution(mesh):
    placed = (
        P(None, ("rows", "cols")),
        P(),
        P(None, ("rows", "cols")),
        P(None, "cols"),
        P(),
        P(),
        P(("rows", "cols"), None, None),
    )
    return jax.shard_map(
        body,
        mesh=mesh,
        in_specs=placed,
        out_specs=(P(None, ("rows", "cols")), P(None, ("rows", "cols"))),
        check_vma=False,
    )
```

profile of v0, /device:TPU:1, one launch (start us, length us, event | category | flops | bytes accessed | tf_op | source)
XLA Modules:
  0.0 1049.2 jit_solution(9034076798608031589)
XLA Ops:
  7.2 0.0 copy-start
  7.2 0.0 all-reduce.12.cloned.1.call-start
  7.2 0.8 fusion.38
  8.1 0.7 compare_and_fusion
  8.8 1.4 fusion.39
  10.8 1.0 copy.9
  13.2 1.5 broadcast_select_fusion
  14.7 7.6 gather_fusion
  22.3 1.1 broadcast_select_fusion.1
  23.4 0.5 copy-done.1
  23.9 2.4 select_bitcast_fusion
  26.3 0.0 all-reduce.12.cloned.1.call-update
  26.3 0.0 all-reduce.6.cloned.1.call-start
  28.3 15.9 %all_gather.3 = bf16[64,2048]{1,0:T(8,128)(2,1)S(1)} all-gather(bf16[64,256]{1,0:T(8,128)(2,1)S(1)} %copy-done.8), channel_id=1, replica_groups=mesh['rows'=32,'cols'=8] {'cols'}, dimensions={1}, use_global_device_ids=true | all-gather | bytes 294912 | tf_op jit(solution)/shard_map/all_gather | solution.py:56
  44.2 249.0 %all-reduce.12.cloned.1.call-done = (f32[16,2048]{0,1:T(8,128)}, f32[16,1024]{0,1:T(8,128)}, f32[16,1024]{0,1:T(8,128)}, f32[16,1024]{0,1:T(8,128)}) async-done(((f32[16,2048]{0,1:T(8,128)}, f32[16,1024]{0,1:T(8,128)}, f32[16,1024]{0,1:T(8,128)}, f32[16,1024]{0,1:T(8,128)}), (f32[16,2048]{0,1:T(8,128)}, f32[16,1024]{0,1:T(8,128)}, f32[16,1024]{0,1:T(8,128)}, ...) | async-done | bytes 327696 | tf_op jit(solution)/shard_map/psum | solution.py:53
  293.2 1.6 multiply_reduce_fusion.4
  294.8 3.1 exponential_convert_fusion.6
  297.9 2.1 exponential_convert_fusion.5
  300.1 2.1 exponential_convert_fusion.4
  302.2 2.1 exponential_convert_fusion.3
  304.3 0.0 copy-start.7
  304.4 0.3 fusion.36
  304.7 0.3 convolution_add_fusion.2
  305.0 0.3 convolution_add_fusion.1
  305.3 0.0 copy-done.7
  305.3 0.3 fusion.7
  305.6 0.0 copy-done
  305.6 1.1 fusion.23
  306.8 0.0 all-reduce.6.cloned.1.call-update
  306.8 0.2 all-reduce.8.cloned.1.call-start
  307.0 0.2 multiply_reduce_fusion.2
  307.2 5.3 exponential_convert_fusion.2
  312.6 0.2 multiply_reduce_fusion.1
  312.8 5.3 exponential_convert_fusion.1
  318.1 229.5 %all-reduce.6.cloned.1.call-done = bf16[64,1024]{1,0:T(8,128)(2,1)} async-done(((bf16[64,1024]{1,0:T(8,128)(2,1)}), bf16[64,1024]{1,0:T(8,128)(2,1)}) %all-reduce.6.cloned.1.call-update) | async-done | bytes 131088 | tf_op jit(solution)/shard_map/psum | solution.py:13
  547.6 2.1 subtract_select_fusion.2
  549.7 1.1 fusion.20
  550.8 0.0 all-reduce.8.cloned.1.call-update
  550.8 0.0 all-reduce.10.cloned.1.call-start
  550.9 1.2 multiply_reduce_fusion
  552.1 240.8 %all-reduce.8.cloned.1.call-done = bf16[64,1024]{1,0:T(8,128)(2,1)} async-done(((bf16[64,1024]{1,0:T(8,128)(2,1)}), bf16[64,1024]{1,0:T(8,128)(2,1)}) %all-reduce.8.cloned.1.call-update) | async-done | bytes 131088 | tf_op jit(solution)/shard_map/psum | solution.py:13
  792.9 2.1 subtract_select_fusion.1
  795.0 1.1 fusion.17
  796.2 0.0 all-reduce.10.cloned.1.call-update
  796.2 6.4 exponential_convert_fusion
  802.7 235.5 %all-reduce.10.cloned.1.call-done = bf16[64,1024]{1,0:T(8,128)(2,1)} async-done(((bf16[64,1024]{1,0:T(8,128)(2,1)}), bf16[64,1024]{1,0:T(8,128)(2,1)}) %all-reduce.10.cloned.1.call-update) | async-done | bytes 131088 | tf_op jit(solution)/shard_map/psum | solution.py:13
  1038.2 1.7 add_select_fusion
  1039.8 2.8 subtract_select_fusion
  (13 shorter events, 0.0 us)
Async XLA Ops:
  7.2 298.4 %copy-start = (bf16[1,1024,1024]{2,1,0:T(8,128)(2,1)S(1)}, bf16[1,1024,1024]{2,1,0:T(8,128)(2,1)}, u32[]{:S(2)}) copy-start(bf16[1,1024,1024]{2,1,0:T(8,128)(2,1)} %param.13) | copy-start | bytes 6291460
  7.2 286.0 %all-reduce.12.cloned.1.call-start = ((), (), s32[]{:S(2)}) async-start(), calls=%async_computation.3 | async-start | bytes 5242880 | tf_op jit(solution)/shard_map/psum | solution.py:53
  22.3 1.6 copy-start.1
  23.9 4.4 copy-start.8
  26.3 521.3 %all-reduce.6.cloned.1.call-start = ((), (), s32[]{:S(2)}) async-start(), calls=%async_computation | async-start | bytes 262144 | tf_op jit(solution)/shard_map/psum | solution.py:13
  293.2 4.7 copy-start.2
  304.3 1.0 copy-start.7
  305.6 1.4 copy-start.4
  306.8 486.2 %all-reduce.8.cloned.1.call-start = ((), (), s32[]{:S(2)}) async-start(), calls=%async_computation.1 | async-start | bytes 262144 | tf_op jit(solution)/shard_map/psum | solution.py:13
  307.2 5.3 copy-start.3
  550.8 487.3 %all-reduce.10.cloned.1.call-start = ((), (), s32[]{:S(2)}) async-start(), calls=%async_computation.2 | async-start | bytes 262144 | tf_op jit(solution)/shard_map/psum | solution.py:13
  796.2 242.0 %copy-start.5 = (bf16[64,1024]{1,0:T(8,128)(2,1)S(1)}, bf16[64,1024]{1,0:T(8,128)(2,1)}, u32[]{:S(2)}) copy-start(bf16[64,1024]{1,0:T(8,128)(2,1)} %all-reduce.6.cloned.1.call-done) | copy-start | bytes 393220
  796.2 242.0 %copy-start.6 = (bf16[64,1024]{1,0:T(8,128)(2,1)S(1)}, bf16[64,1024]{1,0:T(8,128)(2,1)}, u32[]{:S(2)}) copy-start(bf16[64,1024]{1,0:T(8,128)(2,1)} %all-reduce.8.cloned.1.call-done) | copy-start | bytes 393220
Sparse Core Ops, SparseCore 0:
  26.4 266.7 all-reduce.11
  306.9 240.6 all-reduce.5
  554.6 238.3 all-reduce.7
  799.8 238.3 all-reduce.9
where the time goes:
time: 1050 us
  waiting for transfers between devices  955 us (91%)
  matrix products  38.1 us (4%)
  between operations  17.8 us (2%)
  blocking collectives  15.9 us (2%)
  other arithmetic  11.5 us (1%)
  local copies, waits for them, and re-layouts  10.6 us (1%)
    psum x3, waiting for transfers between devices, broadcast(): return lax.psum(jnp.where(mine, value, jnp.zeros_like(value)), axis)  706 us
    psum x1, waiting for transfers between devices, body(): summed = lax.psum(masked, ('rows', 'cols'))  249 us
    dot_general x7, matrix products, kernel_tile(): lax.dot_general(left, right, (((0,), (0,)), ((), ())), precision=lax.Prec...  26.6 us
  transfers between devices with their start and end apart: 4, of which 4 were waited for; matrix products, arithmetic and copies ran while one was open for 2% of the time, Pallas kernels for 0%

commit v1 on v0

v1 whole, which is shorter than its diff:
```python
import functools
import math

import jax
import jax.numpy as jnp
from jax import lax
from jax.experimental import pallas as pl
from jax.experimental.pallas import tpu as pltpu
from jax.sharding import PartitionSpec as P

MESH = pl.DeviceIdType.MESH
noise_var = 0.5
LOG2E = math.log2(math.e)

DIM = 16
COLS = 64
PTS = 1024
STEPS = 3
PLANES = 8
GROUP = 32
INDUCING = 2048
LANES = 128


def split3(x):
    high = x.astype(jnp.bfloat16)
    rest = x - high.astype(jnp.float32)
    mid = rest.astype(jnp.bfloat16)
    low = (rest - mid.astype(jnp.float32)).astype(jnp.bfloat16)
    return high, mid, low


def norm_rows(norm, first):
    parts = [p.astype(jnp.float32) for p in split3(norm)]
    row = lax.broadcasted_iota(jnp.int32, (16, norm.shape[1]), 0)
    one_from = 3 - first
    out = jnp.where((row >= one_from) & (row < one_from + 3), 1.0, 0.0)
    for k in range(3):
        out = jnp.where(row == first + k, parts[k], out)
    return out.astype(jnp.bfloat16)


def left_rows(high, mid, low, x):
    norm = (-0.5 * LOG2E) * jnp.sum(x * x, axis=0, keepdims=True)
    rows = norm_rows(norm, 0)
    return jnp.concatenate([high, high, mid, high, low, mid, rows, jnp.zeros_like(rows)], axis=0)


def right_rows(x):
    norm = (-0.5 * LOG2E) * jnp.sum(x * x, axis=0, keepdims=True)
    high, mid, low = split3(x * LOG2E)
    rows = norm_rows(norm, 3)
    return jnp.concatenate([high, mid, high, low, high, mid, rows, jnp.zeros_like(rows)], axis=0)


def tile_of(left, right):
    power = lax.dot_general(
        left, right, (((0,), (0,)), ((), ())), preferred_element_type=jnp.float32
    )
    return jnp.exp2(power).astype(jnp.bfloat16)


def body(
    pts_ref,
    scale_ref,
    targets_ref,
    own_w_ref,
    index_ref,
    order_ref,
    inverse_ref,
    res_ref,
    wts_ref,
    inverse,
    w_all,
    right,
    a_send,
    a_recv,
    a_mid,
    a_all,
    x_send,
    x_recv,
    x_mid,
    x_all,
    cand,
    d_recv0,
    d_recv1,
    d_recv2,
    d_mid0,
    d_mid1,
    d_mid2,
    d_all,
    ktile,
    local_sem,
    send_sem,
    recv_sem,
):
    d_recv = (d_recv0, d_recv1, d_recv2)
    d_mid = (d_mid0, d_mid1, d_mid2)
    row_id = lax.axis_index("rows")
    col_id = lax.axis_index("cols")
    z = row_id // 4
    spot = (row_id % 4) * 8 + col_id
    me = row_id * 8 + col_id

    def device(plane, place):
        return (plane * 4 + place // 8, place % 8)

    barrier = pltpu.get_barrier_semaphore()

    @pl.loop(1, GROUP)
    def _(k):
        pl.semaphore_signal(
            barrier, inc=1, device_id=device(z, (spot + k) % GROUP), device_id_type=MESH
        )

    @pl.loop(1, PLANES)
    def _(k):
        pl.semaphore_signal(
            barrier, inc=1, device_id=device((z + k) % PLANES, spot), device_id_type=MESH
        )

    get_inverse = pltpu.make_async_copy(inverse_ref.at[0], inverse, local_sem.at[0])
    get_targets = pltpu.make_async_copy(targets_ref, res_ref, local_sem.at[1])
    get_w = pltpu.make_async_copy(own_w_ref, w_all.at[col_id], local_sem.at[2])
    get_w.start()
    get_targets.start()
    get_inverse.start()

    pending = []

    def scatter(phase, src, dst):
        @pl.loop(1, GROUP)
        def _(k):
            place = (spot + k) % GROUP
            pltpu.make_async_remote_copy(
                src_ref=src.at[place],
                dst_ref=dst.at[spot],
                send_sem=send_sem.at[phase],
                recv_sem=recv_sem.at[phase],
                device_id=device(z, place),
                device_id_type=MESH,
            ).start()

        dst[spot] = src[spot]
        return arrival(phase, dst, GROUP - 1, device(z, (spot + 1) % GROUP))

    def arrival(phase, dst, count, other):
        some = dst.at[pl.ds(0, count)]
        all_of_them = pltpu.make_async_remote_copy(
            src_ref=some,
            dst_ref=some,
            send_sem=send_sem.at[phase],
            recv_sem=recv_sem.at[phase],
            device_id=other,
            device_id_type=MESH,
        )
        pending.append(all_of_them)
        return all_of_them

    def along_z(phase, dst):
        @pl.loop(1, PLANES)
        def _(k):
            pltpu.make_async_remote_copy(
                src_ref=dst.at[z],
                dst_ref=dst.at[z],
                send_sem=send_sem.at[phase],
                recv_sem=recv_sem.at[phase],
                device_id=device((z + k) % PLANES, spot),
                device_id_type=MESH,
            ).start()

        return arrival(phase, dst, PLANES - 1, device((z + 1) % PLANES, spot))

    def in_plane(phase, dst):
        @pl.loop(1, GROUP)
        def _(k):
            pltpu.make_async_remote_copy(
                src_ref=dst.at[spot],
                dst_ref=dst.at[spot],
                send_sem=send_sem.at[phase],
                recv_sem=recv_sem.at[phase],
                device_id=device(z, (spot + k) % GROUP),
                device_id_type=MESH,
            ).start()

        return arrival(phase, dst, GROUP - 1, device(z, (spot + 1) % GROUP))

    feature = lax.broadcasted_iota(jnp.int32, (DIM, PTS), 0)
    scales = jnp.zeros((DIM, PTS), jnp.float32)
    for k in range(DIM):
        scales = jnp.where(feature == k, scale_ref[k], scales)
    scaled = pts_ref[...] / scales
    right[...] = right_rows(scaled)
    parts = split3(scaled)
    for p in range(3):
        for g in range(8):
            x_send[p * 8 + g] = parts[p][:, g * LANES : (g + 1) * LANES]
    x_send[pl.ds(24, 8)] = jnp.zeros((8, 16, LANES), jnp.bfloat16)
    stacked = jnp.concatenate(
        [parts[p][:, g * LANES : (g + 1) * LANES] for g in range(8) for p in range(3)], axis=0
    )
    lane_row = lax.broadcasted_iota(jnp.int32, (LANES, LANES), 0)
    local = index_ref[...] - me * PTS
    inside = (local >= 0) & (local < PTS)
    group_of = jnp.where(inside, local >> 7, -1)
    lane_of = local & (LANES - 1)
    for j in range(INDUCING // LANES):
        one_hot = jnp.where(lane_row == lane_of[j : j + 1], 1.0, 0.0).astype(jnp.bfloat16)
        picked = jnp.dot(stacked, one_hot, preferred_element_type=jnp.float32)
        which = jnp.broadcast_to(group_of[j : j + 1], (48, LANES))
        kept = jnp.zeros((48, LANES), jnp.float32)
        for g in range(8):
            kept = jnp.where(which == g, picked[g * 48 : (g + 1) * 48], kept)
        coords = kept[0:16] + kept[16:32] + kept[32:48]
        a_send[j] = coords[0:8]
        a_send[16 + j] = coords[8:16]

    pl.semaphore_wait(barrier, GROUP - 1 + PLANES - 1)

    a1 = scatter(0, a_send, a_recv)
    x1 = scatter(1, x_send, x_recv)
    get_w.wait()

    @pl.loop(1, 8)
    def _(k):
        pltpu.make_async_remote_copy(
            src_ref=w_all.at[col_id],
            dst_ref=w_all.at[col_id],
            send_sem=send_sem.at[2],
            recv_sem=recv_sem.at[2],
            device_id=(row_id, (col_id + k) % 8),
            device_id_type=MESH,
        ).start()

    w1 = arrival(2, w_all, 7, (row_id, (col_id + 1) % 8))

    owners = [order_ref[s] for s in range(STEPS)]
    owner_spot = [o & (GROUP - 1) for o in owners]
    owner_z = [o >> 5 for o in owners]

    a1.wait_recv()
    a_mid[z] = jnp.sum(a_recv[...], axis=0)
    a2 = along_z(3, a_mid)
    x1.wait_recv()
    for s in range(STEPS):
        x_mid[z, s] = x_recv[owner_spot[s]]
    x2 = along_z(4, x_mid)
    a2.wait_recv()
    a_all[spot] = jnp.sum(a_mid[...], axis=0)
    a3 = in_plane(5, a_all)
    x2.wait_recv()
    for s in range(STEPS):
        x_all[spot, s] = x_mid[owner_z[s], s]
    a3.wait_recv()
    x3 = in_plane(6, x_all)

    w1.wait_recv()
    get_targets.wait()

    @pl.loop(0, INDUCING // 256)
    def _(i):
        coords = jnp.concatenate(
            [
                jnp.concatenate([a_all[2 * i], a_all[2 * i + 1]], axis=1),
                jnp.concatenate([a_all[16 + 2 * i], a_all[16 + 2 * i + 1]], axis=1),
            ],
            axis=0,
        )
        left = left_rows(*split3(coords), coords)
        res_ref[...] -= jnp.dot(
            w_all[i], tile_of(left, right[...]), preferred_element_type=jnp.float32
        )

    wts_ref[...] = jnp.zeros_like(wts_ref)
    get_inverse.wait()

    def block_tile(s):
        @pl.loop(0, 4)
        def _(i):
            planes = [
                jnp.concatenate(
                    [x_all[p * 8 + 2 * i, s], x_all[p * 8 + 2 * i + 1, s]], axis=1
                )
                for p in range(3)
            ]
            coords = sum(p.astype(jnp.float32) for p in planes)
            left = left_rows(*planes, coords)
            ktile[s, pl.ds(pl.multiple_of(i * 256, 256), 256), :] = tile_of(left, right[...])

    for s in range(STEPS):
        shifted = res_ref[...].astype(jnp.bfloat16)
        for g in range(4):
            part = jnp.dot(
                shifted,
                inverse[:, g * 256 : (g + 1) * 256],
                preferred_element_type=jnp.float32,
            ).astype(jnp.bfloat16)
            for r in range(4):
                for h in range(2):
                    cand[s, r * 8 + g * 2 + h] = part[
                        r * 16 : (r + 1) * 16, h * LANES : (h + 1) * LANES
                    ]
        d1 = scatter(7 + 3 * s, cand.at[s], d_recv[s])
        if s == 0:
            x3.wait_recv()
            block_tile(0)
        d1.wait_recv()
        d_mid[s][z] = d_recv[s][owner_spot[s]]
        d2 = along_z(8 + 3 * s, d_mid[s])
        if s < STEPS - 1:
            block_tile(s + 1)
        d2.wait_recv()
        d_all[s, spot] = d_mid[s][owner_z[s]]
        d3 = in_plane(9 + 3 * s, d_all.at[s])
        d3.wait_recv()
        delta = jnp.concatenate(
            [
                jnp.concatenate([d_all[s, r * 8 + g] for g in range(8)], axis=1)
                for r in range(4)
            ],
            axis=0,
        )
        mine = (owners[s] == me).astype(jnp.float32)
        delta_f = delta.astype(jnp.float32) * mine
        update = jnp.dot(delta, ktile[s], preferred_element_type=jnp.float32)
        res_ref[...] = (res_ref[...] - update) - noise_var * delta_f
        wts_ref[...] += delta_f

    for transfer in pending:
        transfer.wait_send()


def projected(points, lengthscales, targets, inducing_weights, inducing_index, block_order, block_inverse):
    vmem = pl.BlockSpec(memory_space=pltpu.VMEM)
    smem = pl.BlockSpec(memory_space=pltpu.SMEM)
    anywhere = pl.BlockSpec(memory_space=pl.ANY)
    out = jax.ShapeDtypeStruct((COLS, PTS), jnp.float32)
    bf16, f32 = jnp.bfloat16, jnp.float32
    return pl.pallas_call(
        body,
        out_shape=(out, out),
        in_specs=[vmem, smem, anywhere, anywhere, vmem, smem, anywhere],
        out_specs=(vmem, vmem),
        scratch_shapes=[
            pltpu.VMEM((PTS, PTS), bf16),
            pltpu.VMEM((8, COLS, 256), bf16),
            pltpu.VMEM((LANES, PTS), bf16),
            pltpu.VMEM((GROUP, 8, LANES), f32),
            pltpu.VMEM((GROUP, 8, LANES), f32),
            pltpu.VMEM((PLANES, 8, LANES), f32),
            pltpu.VMEM((GROUP, 8, LANES), f32),
            pltpu.VMEM((GROUP, 16, LANES), bf16),
            pltpu.VMEM((GROUP, 16, LANES), bf16),
            pltpu.VMEM((PLANES, STEPS, 16, LANES), bf16),
            pltpu.VMEM((GROUP, STEPS, 16, LANES), bf16),
            pltpu.VMEM((STEPS, GROUP, 16, LANES), bf16),
            *[pltpu.VMEM((GROUP, 16, LANES), bf16)] * STEPS,
            *[pltpu.VMEM((PLANES, 16, LANES), bf16)] * STEPS,
            pltpu.VMEM((STEPS, GROUP, 16, LANES), bf16),
            pltpu.VMEM((STEPS, PTS, PTS), bf16),
            pltpu.SemaphoreType.DMA((3,)),
            pltpu.SemaphoreType.DMA((16,)),
            pltpu.SemaphoreType.DMA((16,)),
        ],
        compiler_params=pltpu.CompilerParams(
            collective_id=0, has_side_effects=True, vmem_limit_bytes=32 << 20
        ),
        name="projection",
    )(
        points,
        lengthscales,
        targets,
        inducing_weights,
        inducing_index.reshape(INDUCING // LANES, LANES),
        block_order,
        block_inverse,
    )


def solution(mesh):
    placed = (
        P(None, ("rows", "cols")),
        P(),
        P(None, ("rows", "cols")),
        P(None, "cols"),
        P(),
        P(),
        P(("rows", "cols"), None, None),
    )
    return jax.shard_map(
        projected,
        mesh=mesh,
        in_specs=placed,
        out_specs=(P(None, ("rows", "cols")), P(None, ("rows", "cols"))),
        check_vma=False,
    )
```

time: 1050 us -> 87.5 us (0.08)
  waiting for transfers between devices: 955 us -> 0 us
  Pallas kernels: 0 us -> 79 us
  matrix products: 38.1 us -> 0 us
  between operations: 17.8 us -> 0.66 us
  blocking collectives: 15.9 us -> 0 us
  other arithmetic: 11.5 us -> 0 us
    psum x4 -> x0, waiting for transfers between devices: 955 us -> none  [the longest x3 706 us: broadcast(): return lax.psum(jnp.where(mine, value, jnp.zeros_like(value)), axis)]
    pallas_call x0 -> x1, Pallas kernels: none -> 79 us  [projected(): pl.pallas_call(body, out_shape=(out, out), in_specs=[vmem, smem, anywhere...]
    dot_general x17 -> x0, matrix products: 38.1 us -> none  [the longest x7 26.6 us: kernel_tile(): lax.dot_general(left, right, (((0,), (0,)), ((), ())), precision=lax.Prec...]
    all_gather x1 -> x0, blocking collectives: 15.9 us -> none  [body(): shard_part = lax.all_gather(inducing_weights, 'cols', axis=1, tiled=True)]
  transfers between devices with their start and end apart: 4 -> 0, of which waited for: 4 -> 0; matrix products, arithmetic and copies ran while one was open for 2% -> 0% of each run, Pallas kernels for 0% -> 0%
where the time goes in v1:
time: 87.5 us; the launch traced here: 87.2 us
  Pallas kernels  79 us (90%)
  local copies, waits for them, and re-layouts  7.54 us (9%)
    pallas_call x1, Pallas kernels, projected(): pl.pallas_call(body, out_shape=(out, out), in_specs=[vmem, smem, anywhere...  79 us
    unnamed x16, local copies, waits for them, and re-layouts  7.54 us

profile of v1, /device:TPU:1, one launch (start us, length us, event | category | flops | bytes accessed | tf_op | source)
XLA Modules:
  0.0 87.2 jit_solution(10514404126614901717)
XLA Ops:
  0.6 0.0 copy-start
  0.6 1.6 %copy-done = bf16[1,1024,1024]{2,1,0:T(8,128)(2,1)S(1)} copy-done((bf16[1,1024,1024]{2,1,0:T(8,128)(2,1)S(1)}, bf16[1,1024,1024]{2,1,0:T(8,128)(2,1)}, u32[]{:S(2)}) %copy-start) | copy-done | bytes 2097176
  2.2 0.0 copy-start.1
  2.2 0.9 %copy-done.1 = f32[64,1024]{1,0:T(8,128)S(1)} copy-done((f32[64,1024]{1,0:T(8,128)S(1)}, f32[64,1024]{1,0:T(8,128)}, u32[]{:S(2)}) %copy-start.1) | copy-done | bytes 262168
  3.2 0.0 copy-start.2
  3.2 0.8 copy-done.2
  4.0 0.0 copy-start.3
  4.0 0.8 copy-done.3
  4.8 0.0 copy-start.4
  4.8 0.7 copy-done.4
  5.5 0.0 copy-start.5
  5.5 0.7 copy-done.5
  6.1 0.0 copy-start.6
  6.1 0.7 copy-done.6
  6.8 79.0 %projection.1 = (f32[64,1024]{1,0:T(8,128)S(1)}, f32[64,1024]{1,0:T(8,128)S(1)}) custom-call(f32[16,1024]{1,0:T(8,128)S(1)} %copy-done.2, f32[16]{0:T(128)S(1)} %copy-done.5, f32[64,1024]{1,0:T(8,128)S(1)} %copy-done.1, bf16[64,256]{1,0:T(8,128)(2,1)S(1)} %copy-done.3, s32[16,128]{1,0:T(8,128)S(1)} %bitcast.1, s32[3]{0:T(128)S(1)} %copy-done.6, ...), custom_call_target="tpu_custom_call" | custom-call | tf_op jit(solution)/shard_map/projection/pallas_call | solution.py:339
  85.8 0.7 copy.11
  86.5 0.7 copy.12
Async XLA Ops:
  0.6 1.6 %copy-start = (bf16[1,1024,1024]{2,1,0:T(8,128)(2,1)S(1)}, bf16[1,1024,1024]{2,1,0:T(8,128)(2,1)}, u32[]{:S(2)}) copy-start(bf16[1,1024,1024]{2,1,0:T(8,128)(2,1)} %inverse_ref.1) | copy-start | bytes 6291460
  2.2 0.9 %copy-start.1 = (f32[64,1024]{1,0:T(8,128)S(1)}, f32[64,1024]{1,0:T(8,128)}, u32[]{:S(2)}) copy-start(f32[64,1024]{1,0:T(8,128)} %targets_ref.1) | copy-start | bytes 786436
  3.2 0.8 copy-start.2
  4.0 0.8 copy-start.3
  4.8 0.7 copy-start.4
  5.5 0.7 copy-start.5
  6.1 0.7 copy-start.6

commit v2 on v1

--- a/solution.py
+++ b/solution.py
@@ -61,15 +61,19 @@
 
 
 def body(
-    pts_ref,
-    scale_ref,
+    pts_hbm,
+    scale_hbm,
     targets_ref,
     own_w_ref,
-    index_ref,
-    order_ref,
+    index_hbm,
+    order_hbm,
     inverse_ref,
     res_ref,
     wts_ref,
+    pts_ref,
+    scale_ref,
+    index_ref,
+    order_ref,
     inverse,
     w_all,
     right,
@@ -122,6 +126,19 @@
     get_inverse = pltpu.make_async_copy(inverse_ref.at[0], inverse, local_sem.at[0])
     get_targets = pltpu.make_async_copy(targets_ref, res_ref, local_sem.at[1])
     get_w = pltpu.make_async_copy(own_w_ref, w_all.at[col_id], local_sem.at[2])
+    small = [
+        pltpu.make_async_copy(src, dst, local_sem.at[3 + k])
+        for k, (src, dst) in enumerate(
+            [
+                (pts_hbm, pts_ref),
+                (scale_hbm, scale_ref),
+                (index_hbm, index_ref),
+                (order_hbm, order_ref),
+            ]
+        )
+    ]
+    for copy in small:
+        copy.start()
     get_w.start()
     get_targets.start()
     get_inverse.start()
@@ -185,6 +202,8 @@
 
         return arrival(phase, dst, GROUP - 1, device(z, (spot + 1) % GROUP))
 
+    for copy in small:
+        copy.wait()
     feature = lax.broadcasted_iota(jnp.int32, (DIM, PTS), 0)
     scales = jnp.zeros((DIM, PTS), jnp.float32)
     for k in range(DIM):
@@ -257,8 +276,8 @@
     w1.wait_recv()
     get_targets.wait()
 
-    @pl.loop(0, INDUCING // 256)
-    def _(i):
+    warm = jnp.zeros((COLS, PTS), jnp.float32)
+    for i in range(INDUCING // 256):
         coords = jnp.concatenate(
             [
                 jnp.concatenate([a_all[2 * i], a_all[2 * i + 1]], axis=1),
@@ -267,9 +286,10 @@
             axis=0,
         )
         left = left_rows(*split3(coords), coords)
-        res_ref[...] -= jnp.dot(
+        warm += jnp.dot(
             w_all[i], tile_of(left, right[...]), preferred_element_type=jnp.float32
         )
+    res_ref[...] -= warm
 
     wts_ref[...] = jnp.zeros_like(wts_ref)
     get_inverse.wait()
@@ -332,16 +352,19 @@
 
 def projected(points, lengthscales, targets, inducing_weights, inducing_index, block_order, block_inverse):
     vmem = pl.BlockSpec(memory_space=pltpu.VMEM)
-    smem = pl.BlockSpec(memory_space=pltpu.SMEM)
-    anywhere = pl.BlockSpec(memory_space=pl.ANY)
+    hbm = pl.BlockSpec(memory_space=pltpu.HBM)
     out = jax.ShapeDtypeStruct((COLS, PTS), jnp.float32)
     bf16, f32 = jnp.bfloat16, jnp.float32
     return pl.pallas_call(
         body,
         out_shape=(out, out),
-        in_specs=[vmem, smem, anywhere, anywhere, vmem, smem, anywhere],
+        in_specs=[hbm] * 7,
         out_specs=(vmem, vmem),
         scratch_shapes=[
+            pltpu.VMEM((DIM, PTS), f32),
+            pltpu.SMEM((DIM,), f32),
+            pltpu.VMEM((INDUCING // LANES, LANES), jnp.int32),
+            pltpu.SMEM((STEPS,), jnp.int32),
             pltpu.VMEM((PTS, PTS), bf16),
             pltpu.VMEM((8, COLS, 256), bf16),
             pltpu.VMEM((LANES, PTS), bf16),
@@ -358,12 +381,12 @@
             *[pltpu.VMEM((PLANES, 16, LANES), bf16)] * STEPS,
             pltpu.VMEM((STEPS, GROUP, 16, LANES), bf16),
             pltpu.VMEM((STEPS, PTS, PTS), bf16),
-            pltpu.SemaphoreType.DMA((3,)),
+            pltpu.SemaphoreType.DMA((7,)),
             pltpu.SemaphoreType.DMA((16,)),
             pltpu.SemaphoreType.DMA((16,)),
         ],
         compiler_params=pltpu.CompilerParams(
-            collective_id=0, has_side_effects=True, vmem_limit_bytes=32 << 20
+            collective_id=0, has_side_effects=True, vmem_limit_bytes=62 << 20
         ),
         name="projection",
     )(

time: 87.5 us -> 83.8 us (0.958)
  local copies, waits for them, and re-layouts: 7.54 us -> 3.34 us
    unnamed x16 -> x2, local copies, waits for them, and re-layouts: 7.54 us -> 3.34 us
where the time goes in v2:
time: 83.8 us; the launch traced here: 83.6 us
  Pallas kernels  79.6 us (95%)
  local copies, waits for them, and re-layouts  3.34 us (4%)
    pallas_call x1, Pallas kernels, projected(): pl.pallas_call(body, out_shape=(out, out), in_specs=[hbm] * 7, out_specs=...  79.6 us
    unnamed x2, local copies, waits for them, and re-layouts  3.34 us

profile of v2, /device:TPU:1, one launch (start us, length us, event | category | flops | bytes accessed | tf_op | source)
XLA Modules:
  0.0 83.6 jit_solution(10913289863413172069)
XLA Ops:
  0.6 79.6 %projection.1 = (f32[64,1024]{1,0:T(8,128)}, f32[64,1024]{1,0:T(8,128)}) custom-call(f32[16,1024]{1,0:T(8,128)} %pts_hbm.1, f32[16]{0:T(128)} %scale_hbm.1, f32[64,1024]{1,0:T(8,128)} %targets_ref.1, bf16[64,256]{1,0:T(8,128)(2,1)} %own_w_ref.1, s32[16,128]{1,0:T(8,128)} %bitcast.1, s32[3]{0:T(128)} %order_hbm.1, bf16[1,1024,1024]{2,1,0:T(8,128)(2,1)} %inverse_ref.1), custom_call_target="tpu_custom_call" | custom-call | tf_op jit(solution)/shard_map/projection/pallas_call | solution.py:358
  80.3 1.7 %copy.11 = f32[64,1024]{1,0:T(8,128)} copy(f32[64,1024]{1,0:T(8,128)} %get-tuple-element.4) | data formatting | bytes 524288
  82.0 1.7 %copy.12 = f32[64,1024]{1,0:T(8,128)} copy(f32[64,1024]{1,0:T(8,128)} %get-tuple-element.5) | data formatting | bytes 524288

commit v3 on v2

--- a/solution.py
+++ b/solution.py
@@ -20,6 +20,13 @@
 GROUP = 32
 INDUCING = 2048
 LANES = 128
+
+
+PLANE_ORDER = sorted(
+    [(dx, dy, dc) for dx in range(4) for dy in range(4) for dc in range(2) if dx or dy or dc],
+    key=lambda o: (-(min(o[0], 4 - o[0]) + min(o[1], 4 - o[1])), o[0] % 2, o[2], o[0], o[1]),
+)
+PLANE_STEPS = (4, 3, 5, 2, 6, 1, 7)
 
 
 def split3(x):
@@ -106,22 +113,25 @@
     spot = (row_id % 4) * 8 + col_id
     me = row_id * 8 + col_id
 
-    def device(plane, place):
-        return (plane * 4 + place // 8, place % 8)
+    x_pos, y_pos, core = row_id % 4, col_id // 2, col_id % 2
+    xs = [x_pos] + [(x_pos + d) % 4 for d in (1, 2, 3)]
+    ys = [y_pos] + [(y_pos + d) % 4 for d in (1, 2, 3)]
+    cores = (core, 1 - core)
+    others = []
+    for dx, dy, dc in PLANE_ORDER:
+        others.append(
+            (
+                xs[dx] * 8 + ys[dy] * 2 + cores[dc],
+                (z * 4 + xs[dx], ys[dy] * 2 + cores[dc]),
+            )
+        )
+    planes = [(((z + k) % PLANES) * 4 + x_pos, col_id) for k in PLANE_STEPS]
 
     barrier = pltpu.get_barrier_semaphore()
-
-    @pl.loop(1, GROUP)
-    def _(k):
-        pl.semaphore_signal(
-            barrier, inc=1, device_id=device(z, (spot + k) % GROUP), device_id_type=MESH
-        )
-
-    @pl.loop(1, PLANES)
-    def _(k):
-        pl.semaphore_signal(
-            barrier, inc=1, device_id=device((z + k) % PLANES, spot), device_id_type=MESH
-        )
+    for _, place in others:
+        pl.semaphore_signal(barrier, inc=1, device_id=place, device_id_type=MESH)
+    for place in planes:
+        pl.semaphore_signal(barrier, inc=1, device_id=place, device_id_type=MESH)
 
     get_inverse = pltpu.make_async_copy(inverse_ref.at[0], inverse, local_sem.at[0])
     get_targets = pltpu.make_async_copy(targets_ref, res_ref, local_sem.at[1])
@@ -145,21 +155,15 @@
 
     pending = []
 
-    def scatter(phase, src, dst):
-        @pl.loop(1, GROUP)
-        def _(k):
-            place = (spot + k) % GROUP
-            pltpu.make_async_remote_copy(
-                src_ref=src.at[place],
-                dst_ref=dst.at[spot],
-                send_sem=send_sem.at[phase],
-                recv_sem=recv_sem.at[phase],
-                device_id=device(z, place),
-                device_id_type=MESH,
-            ).start()
-
-        dst[spot] = src[spot]
-        return arrival(phase, dst, GROUP - 1, device(z, (spot + 1) % GROUP))
+    def send(phase, src, dst, place):
+        pltpu.make_async_remote_copy(
+            src_ref=src,
+            dst_ref=dst,
+            send_sem=send_sem.at[phase],
+            recv_sem=recv_sem.at[phase],
+            device_id=place,
+            device_id_type=MESH,
+        ).start()
 
     def arrival(phase, dst, count, other):
         some = dst.at[pl.ds(0, count)]
@@ -174,33 +178,21 @@
         pending.append(all_of_them)
         return all_of_them
 
+    def scatter(phase, src, dst):
+        for there, place in others:
+            send(phase, src.at[there], dst.at[spot], place)
+        dst[spot] = src[spot]
+        return arrival(phase, dst, GROUP - 1, others[0][1])
+
     def along_z(phase, dst):
-        @pl.loop(1, PLANES)
-        def _(k):
-            pltpu.make_async_remote_copy(
-                src_ref=dst.at[z],
-                dst_ref=dst.at[z],
-                send_sem=send_sem.at[phase],
-                recv_sem=recv_sem.at[phase],
-                device_id=device((z + k) % PLANES, spot),
-                device_id_type=MESH,
-            ).start()
-
-        return arrival(phase, dst, PLANES - 1, device((z + 1) % PLANES, spot))
+        for place in planes:
+            send(phase, dst.at[z], dst.at[z], place)
+        return arrival(phase, dst, PLANES - 1, planes[0])
 
     def in_plane(phase, dst):
-        @pl.loop(1, GROUP)
-        def _(k):
-            pltpu.make_async_remote_copy(
-                src_ref=dst.at[spot],
-                dst_ref=dst.at[spot],
-                send_sem=send_sem.at[phase],
-                recv_sem=recv_sem.at[phase],
-                device_id=device(z, (spot + k) % GROUP),
-                device_id_type=MESH,
-            ).start()
-
-        return arrival(phase, dst, GROUP - 1, device(z, (spot + 1) % GROUP))
+        for _, place in others:
+            send(phase, dst.at[spot], dst.at[spot], place)
+        return arrival(phase, dst, GROUP - 1, others[0][1])
 
     for copy in small:
         copy.wait()
@@ -237,21 +229,10 @@
     pl.semaphore_wait(barrier, GROUP - 1 + PLANES - 1)
 
     a1 = scatter(0, a_send, a_recv)
-    x1 = scatter(1, x_send, x_recv)
     get_w.wait()
-
-    @pl.loop(1, 8)
-    def _(k):
-        pltpu.make_async_remote_copy(
-            src_ref=w_all.at[col_id],
-            dst_ref=w_all.at[col_id],
-            send_sem=send_sem.at[2],
-            recv_sem=recv_sem.at[2],
-            device_id=(row_id, (col_id + k) % 8),
-            device_id_type=MESH,
-        ).start()
-
-    w1 = arrival(2, w_all, 7, (row_id, (col_id + 1) % 8))
+    siblings = [o for o, (dx, _, _) in zip(others, PLANE_ORDER) if dx == 0]
+    for _, place in siblings[:3]:
+        send(2, w_all.at[col_id], w_all.at[col_id], place)
 
     owners = [order_ref[s] for s in range(STEPS)]
     owner_spot = [o & (GROUP - 1) for o in owners]
@@ -260,18 +241,18 @@
     a1.wait_recv()
     a_mid[z] = jnp.sum(a_recv[...], axis=0)
     a2 = along_z(3, a_mid)
+    for _, place in siblings[3:]:
+        send(2, w_all.at[col_id], w_all.at[col_id], place)
+    w1 = arrival(2, w_all, 7, siblings[0][1])
+    x1 = scatter(1, x_send, x_recv)
+    a2.wait_recv()
+    a_all[spot] = jnp.sum(a_mid[...], axis=0)
+    a3 = in_plane(5, a_all)
     x1.wait_recv()
     for s in range(STEPS):
         x_mid[z, s] = x_recv[owner_spot[s]]
     x2 = along_z(4, x_mid)
-    a2.wait_recv()
-    a_all[spot] = jnp.sum(a_mid[...], axis=0)
-    a3 = in_plane(5, a_all)
-    x2.wait_recv()
-    for s in range(STEPS):
-        x_all[spot, s] = x_mid[owner_z[s], s]
     a3.wait_recv()
-    x3 = in_plane(6, x_all)
 
     w1.wait_recv()
     get_targets.wait()
@@ -295,17 +276,16 @@
     get_inverse.wait()
 
     def block_tile(s):
-        @pl.loop(0, 4)
-        def _(i):
-            planes = [
+        for i in range(4):
+            planes_of = [
                 jnp.concatenate(
-                    [x_all[p * 8 + 2 * i, s], x_all[p * 8 + 2 * i + 1, s]], axis=1
+                    [x_all[s, p * 8 + 2 * i], x_all[s, p * 8 + 2 * i + 1]], axis=1
                 )
                 for p in range(3)
             ]
-            coords = sum(p.astype(jnp.float32) for p in planes)
-            left = left_rows(*planes, coords)
-            ktile[s, pl.ds(pl.multiple_of(i * 256, 256), 256), :] = tile_of(left, right[...])
+            coords = sum(p.astype(jnp.float32) for p in planes_of)
+            left = left_rows(*planes_of, coords)
+            ktile[i * 256 : (i + 1) * 256, :] = tile_of(left, right[...])
 
     for s in range(STEPS):
         shifted = res_ref[...].astype(jnp.bfloat16)
@@ -320,18 +300,19 @@
                     cand[s, r * 8 + g * 2 + h] = part[
                         r * 16 : (r + 1) * 16, h * LANES : (h + 1) * LANES
                     ]
-        d1 = scatter(7 + 3 * s, cand.at[s], d_recv[s])
+        d1 = scatter(7 + 4 * s, cand.at[s], d_recv[s])
         if s == 0:
-            x3.wait_recv()
-            block_tile(0)
+            x2.wait_recv()
         d1.wait_recv()
         d_mid[s][z] = d_recv[s][owner_spot[s]]
-        d2 = along_z(8 + 3 * s, d_mid[s])
-        if s < STEPS - 1:
-            block_tile(s + 1)
+        d2 = along_z(8 + 4 * s, d_mid[s])
+        x_all[s, spot] = x_mid[owner_z[s], s]
+        x3 = in_plane(10 + 4 * s, x_all.at[s])
         d2.wait_recv()
         d_all[s, spot] = d_mid[s][owner_z[s]]
-        d3 = in_plane(9 + 3 * s, d_all.at[s])
+        d3 = in_plane(9 + 4 * s, d_all.at[s])
+        x3.wait_recv()
+        block_tile(s)
         d3.wait_recv()
         delta = jnp.concatenate(
             [
@@ -342,7 +323,7 @@
         )
         mine = (owners[s] == me).astype(jnp.float32)
         delta_f = delta.astype(jnp.float32) * mine
-        update = jnp.dot(delta, ktile[s], preferred_element_type=jnp.float32)
+        update = jnp.dot(delta, ktile[...], preferred_element_type=jnp.float32)
         res_ref[...] = (res_ref[...] - update) - noise_var * delta_f
         wts_ref[...] += delta_f
 
@@ -353,7 +334,7 @@
 def projected(points, lengthscales, targets, inducing_weights, inducing_index, block_order, block_inverse):
     vmem = pl.BlockSpec(memory_space=pltpu.VMEM)
     hbm = pl.BlockSpec(memory_space=pltpu.HBM)
-    out = jax.ShapeDtypeStruct((COLS, PTS), jnp.float32)
+    out = pltpu.VMEM((COLS, PTS), jnp.float32)
     bf16, f32 = jnp.bfloat16, jnp.float32
     return pl.pallas_call(
         body,
@@ -375,15 +356,15 @@
             pltpu.VMEM((GROUP, 16, LANES), bf16),
             pltpu.VMEM((GROUP, 16, LANES), bf16),
             pltpu.VMEM((PLANES, STEPS, 16, LANES), bf16),
-            pltpu.VMEM((GROUP, STEPS, 16, LANES), bf16),
+            pltpu.VMEM((STEPS, GROUP, 16, LANES), bf16),
             pltpu.VMEM((STEPS, GROUP, 16, LANES), bf16),
             *[pltpu.VMEM((GROUP, 16, LANES), bf16)] * STEPS,
             *[pltpu.VMEM((PLANES, 16, LANES), bf16)] * STEPS,
             pltpu.VMEM((STEPS, GROUP, 16, LANES), bf16),
-            pltpu.VMEM((STEPS, PTS, PTS), bf16),
+            pltpu.VMEM((PTS, PTS), bf16),
             pltpu.SemaphoreType.DMA((7,)),
-            pltpu.SemaphoreType.DMA((16,)),
-            pltpu.SemaphoreType.DMA((16,)),
+            pltpu.SemaphoreType.DMA((19,)),
+            pltpu.SemaphoreType.DMA((19,)),
         ],
         compiler_params=pltpu.CompilerParams(
             collective_id=0, has_side_effects=True, vmem_limit_bytes=62 << 20

time: 83.8 us -> 74.4 us (0.89)
  Pallas kernels: 79.6 us -> 72.3 us
  local copies, waits for them, and re-layouts: 3.34 us -> 1.41 us
    pallas_call x1, Pallas kernels: 79.6 us -> 72.3 us  [projected(): pl.pallas_call(body, out_shape=(out, out), in_specs=[hbm] * 7, out_specs=...]
    unnamed x2, local copies, waits for them, and re-layouts: 3.34 us -> 1.41 us
where the time goes in v3:
time: 74.4 us; the launch traced here: 74.3 us
  Pallas kernels  72.3 us (97%)
  local copies, waits for them, and re-layouts  1.41 us (2%)
    pallas_call x1, Pallas kernels, projected(): pl.pallas_call(body, out_shape=(out, out), in_specs=[hbm] * 7, out_specs=...  72.3 us

profile of v3, /device:TPU:1, one launch (start us, length us, event | category | flops | bytes accessed | tf_op | source)
XLA Modules:
  0.0 74.3 jit_solution(17534921907896956840)
XLA Ops:
  0.6 72.3 %projection.1 = (f32[64,1024]{1,0:T(8,128)S(1)}, f32[64,1024]{1,0:T(8,128)S(1)}) custom-call(f32[16,1024]{1,0:T(8,128)} %pts_hbm.1, f32[16]{0:T(128)} %scale_hbm.1, f32[64,1024]{1,0:T(8,128)} %targets_ref.1, bf16[64,256]{1,0:T(8,128)(2,1)} %own_w_ref.1, s32[16,128]{1,0:T(8,128)} %bitcast.1, s32[3]{0:T(128)} %order_hbm.1, bf16[1,1024,1024]{2,1,0:T(8,128)(2,1)} %inverse_ref.1), custom_call_target="tpu_custom_call" | custom-call | tf_op jit(solution)/shard_map/projection/pallas_call | solution.py:339
  72.9 0.7 copy.11
  73.6 0.7 copy.12
